TPU v7x, 256 devices: a whole 4x4x8 slice. The times are simulated.
256 devices in a mesh: blk: 16 (over y_hi, z), frames: 16 (over x, y_lo, core).
Axes of the slice: x: 4, y: 4 (y_hi: 2, y_lo: 2; y = y_hi * 2 + y_lo), z: 8, core: 2. Of those that a mesh axis runs over, the one named last changes fastest.
Arguments:
- coarse_query: bfloat16 [512, 16, 256], P('blk'), may hold values from -125 to 125
- coarse_feat: bfloat16 [64, 8160, 256], P('frames', 'blk'), may hold values from -61 to 61
- fine_query: bfloat16 [512, 128], P(('blk', 'frames')), may hold values from -175 to 175
- fine_tiles: bfloat16 [64, 1024, 64, 128], P('frames', 'blk'), may hold values from -61 to 61
- track_pos: int32 [2, 64, 512], P(None, None, ('blk', 'frames')), may hold values from 0 to 959, as said below
- tile_list: int32 [64, 16, 16, 8], P('frames', 'blk'), may hold values from 0 to 63, as said below
- tile_valid: int32 [64, 16, 16, 8], P('frames', 'blk'), may hold values from 0 to 1, as said below
Outputs:
- coarse_pos: float32 [2, 64, 512], P(None, 'frames', 'blk')
- fine_offset: float32 [2, 64, 512], P(None, None, ('blk', 'frames'))
Inputs may be any that keep to these rules, and one draw needn't show every extreme that they name: `tile_list`: in each list the valid slots come first and name distinct tiles of the group's window; padded slots hold 63; in every frame and group some owner's list is full. `tile_valid`: each list has at least 4 valid slots. `track_pos`: rows lie below 544 and columns below 960.
All inputs are finite; a program needn't handle non-finite values.
Results may differ from a plain program's by a relative error of at most 0.0003.
Values may be sent and summed in bfloat16 or wider, within the bound.
A program may use at most 192 MiB of HBM per device.

v0:
```python
import math
import jax
import jax.numpy as jnp
from jax import lax
from jax.sharding import PartitionSpec as P

GH = 68
GW = 120
TILE = 8
SPREAD = 32.0


def coarse(coarse_query, coarse_feat):
    track_group, heads, channels = coarse_query.shape
    frames_here, region, _ = coarse_feat.shape
    blocks = lax.axis_size("blk")
    scale = 1.0 / math.sqrt(channels)
    start = lax.axis_index("blk") * region
    queries = lax.all_gather(coarse_query.reshape(track_group * heads, channels), "blk", axis=0)
    positions = start + jnp.arange(region, dtype=jnp.int32)
    pos_row = (positions // GW).astype(jnp.float32)
    pos_col = (positions % GW).astype(jnp.float32)
    scores = (
        jnp.einsum("brc,fpc->bfpr", queries, coarse_feat, preferred_element_type=jnp.float32)
        * scale
    )
    top = jnp.max(scores, axis=2)
    weights = jnp.exp(scores - top[:, :, None])
    stats = jnp.stack(
        [
            top,
            jnp.sum(weights, axis=2),
            jnp.sum(weights * pos_row[None, None, :, None], axis=2),
            jnp.sum(weights * pos_col[None, None, :, None], axis=2),
        ],
        axis=1,
    )
    stats = lax.all_to_all(stats, "blk", split_axis=0, concat_axis=0, tiled=True)
    top = jnp.max(stats[:, 0], axis=0, keepdims=True)
    factor = jnp.exp(stats[:, 0] - top)
    total = jnp.sum(stats[:, 1] * factor, axis=0)
    rows = jnp.sum(stats[:, 2] * factor, axis=0) / total
    cols = jnp.sum(stats[:, 3] * factor, axis=0) / total
    rows = jnp.mean(rows.reshape(frames_here, track_group, heads), axis=2)
    cols = jnp.mean(cols.reshape(frames_here, track_group, heads), axis=2)
    return jnp.stack([(rows - (GH - 1) / 2.0) / (GH / 4.0), (cols - (GW - 1) / 2.0) / (GW / 4.0)])


def fine(fine_query, fine_tiles, track_pos, tile_list, tile_valid, region):
    frames_here, tiles, cells, channels = fine_tiles.shape
    owners = tile_list.shape[2]
    owned = fine_query.shape[0]
    start = lax.axis_index("blk") * region
    descs = lax.all_gather(fine_query, "frames", axis=0, tiled=True)
    places = lax.all_to_all(track_pos, "frames", split_axis=1, concat_axis=2, tiled=True).astype(
        jnp.float32
    )
    scores = jnp.einsum(
        "nc,fkc->fnk",
        descs,
        fine_tiles.reshape(frames_here, tiles * cells, channels),
        preferred_element_type=jnp.float32,
    ) * (1.0 / math.sqrt(channels))
    ids = tile_list[:, 0]
    live = tile_valid[:, 0]
    listed = jnp.any((ids[:, :, :, None] == jnp.arange(tiles)) & (live[:, :, :, None] > 0), axis=2)
    listed = jnp.repeat(jnp.repeat(listed, owned, axis=1), cells, axis=2)
    index = jnp.arange(tiles * cells, dtype=jnp.int32)
    cell = start + index // cells
    inner = index % cells
    row = (cell // GW * TILE + inner // TILE).astype(jnp.float32)
    col = (cell % GW * TILE + inner % TILE).astype(jnp.float32)
    away_row = row - places[0][:, :, None]
    away_col = col - places[1][:, :, None]
    scores = scores - (away_row**2 + away_col**2) * (0.5 / (SPREAD * SPREAD))
    scores = jnp.where(listed, scores, -1e30)
    weights = jnp.exp(scores - jnp.max(scores, axis=2, keepdims=True))
    total = jnp.sum(weights, axis=2)
    out = jnp.stack(
        [
            jnp.sum(weights * away_row, axis=2) / total / SPREAD,
            jnp.sum(weights * away_col, axis=2) / total / SPREAD,
        ]
    )
    return lax.all_to_all(out, "frames", split_axis=2, concat_axis=1, tiled=True)


def body(coarse_query, coarse_feat, fine_query, fine_tiles, track_pos, tile_list, tile_valid):
    offset = fine(fine_query, fine_tiles, track_pos, tile_list, tile_valid, coarse_feat.shape[1])
    return (coarse(coarse_query, coarse_feat), offset)


def solution(mesh):
    return jax.shard_map(
        body,
        mesh=mesh,
        in_specs=(
            P("blk", None, None),
            P("frames", "blk", None),
            P(("blk", "frames"), None),
            P("frames", "blk", None, None),
            P(None, None, ("blk", "frames")),
            P("frames", "blk", None, None),
            P("frames", "blk", None, None),
        ),
        out_specs=(P(None, "frames", "blk"), P(None, None, ("blk", "frames"))),
        check_vma=False,
    )
```

profile of v0, /device:TPU:2, one launch (start us, length us, event | category | flops | bytes accessed | tf_op | source)
XLA Modules:
  0.0 203.0 jit_solution(1856049340781756826)
XLA Ops:
  7.2 0.7 all-gather.3.cloned.1.call-update
  7.9 1.4 copy.87
  9.3 5.9 %all-to-all-start.1 = ((s32[2,64,2]{2,0,1:T(2,128)}), s32[2,64,2]{2,0,1:T(2,128)S(1)}, u32[]{:S(2)}, u32[]{:S(2)}) async-start(s32[2,64,2]{2,0,1:T(2,128)} %copy.87), calls=%async_computation.1 | async-start | bytes 131072 | tf_op jit(solution)/shard_map/all_to_all | solution.py:55
  15.2 0.8 copy.83
  16.0 0.7 compare_bitcast_fusion
  16.7 0.1 copy.84
  16.8 0.2 fusion.16
  17.1 17.5 %all-gather = bf16[16,2,128]{2,1,0:T(2,128)(2,1)S(1)} all-gather(bf16[1,2,128]{2,1,0:T(2,128)(2,1)} %bitcast.111), channel_id=1, replica_groups=mesh['blk'=16,'frames'=16] {'frames'}, dimensions={0}, use_global_device_ids=true | all-gather | bytes 8704 | tf_op jit(solution)/shard_map/all_gather | solution.py:54
  34.6 1.4 broadcast_in_dim.9
  36.0 2.6 %reshape.202 = pred[4,32,4096]{2,1,0:T(32,128)(4,1)S(1)} reshape(pred[4,32,64,64]{3,2,1,0:T(32,128)(4,1)S(1)} %broadcast_in_dim.9) | data formatting | bytes 1048576 | tf_op jit(solution)/shard_map/reshape | solution.py:67
  38.7 0.1 convert_element_type.42
  39.0 4.6 %fusion.12 = (f32[4,32]{1,0:T(4,128)S(1)}, f32[4,32]{1,0:T(4,128)S(1)}, f32[4,32]{1,0:T(4,128)S(1)}) fusion(f32[4,32]{1,0:T(4,128)S(1)} %copy.90, f32[4096]{0:T(1024)S(1)} %get-tuple-element.19, f32[4,32]{1,0:T(4,128)S(1)} %copy.92, f32[4096]{0:T(1024)S(1)} %get-tuple-element.20, pred[4,32,4096]{2,1,0:T(32,128)(4,1)S(1)} %reshape.202, ...), kind=kOutput, calls=%fused_computation.21 | convolution fusion | flops 143134464 | bytes 4762112 | tf_op jit(solution)/shard_map/sub | solution.py:77
  43.6 0.7 copy.93
  44.3 6.0 %all-to-all-start.2 = ((f32[2,4,32]{1,0,2:T(2,128)}), f32[2,4,32]{1,0,2:T(2,128)S(1)}, u32[]{:S(2)}, u32[]{:S(2)}) async-start(f32[2,4,32]{1,0,2:T(2,128)} %copy.93), calls=%async_computation.2 | async-start | bytes 65536 | tf_op jit(solution)/shard_map/all_to_all | solution.py:85
  50.3 63.3 %all-gather.3.cloned.1.call-done = bf16[16,512,256]{2,1,0:T(8,128)(2,1)} async-done(((bf16[1,512,256]{2,1,0:T(8,128)(2,1)}), bf16[16,512,256]{2,1,0:T(8,128)(2,1)}) %all-gather.3.cloned.1.call-update) | async-done | bytes 4194320 | tf_op jit(solution)/shard_map/all_gather | solution.py:19
  113.6 25.3 %bitcast_reduce_fusion = (f32[16,4,512]{2,0,1:T(8,128)S(1)}, f32[4,510,16,512]{3,1,2,0:T(8,128)}) fusion(bf16[16,512,256]{2,1,0:T(8,128)(2,1)} %all-gather.3.cloned.1.call-done, bf16[4,510,256,1]{2,0,1,3:T(4,128)(2,1)S(1)} %bitcast.99), kind=kOutput, calls=%fused_computation.2 | convolution fusion | flops 8589770752 | bytes 72216576 | tf_op jit(solution)/shard_map/brc,fpc->bfpr/dot_general | solution.py:24
  138.9 36.5 %fusion.2 = (f32[16,4,512]{2,0,1:T(8,128)S(1)}, f32[16,4,512]{2,0,1:T(8,128)S(1)}, f32[16,4,512]{2,0,1:T(8,128)S(1)}) fusion(f32[4,510,16,512]{3,1,2,0:T(8,128)} %get-tuple-element.18, f32[16,4,512]{2,0,1:T(8,128)S(1)} %get-tuple-element.17, f32[510]{0:T(512)S(1)} %get-tuple-element.22, f32[510]{0:T(512)S(1)} %get-tuple-element.21), kind=kLoop, calls=%fused_computation.6 | loop fusion | flops 116883456 | bytes 67375088 | tf_op jit(solution)/shard_map/reduce_sum | solution.py:32
  175.5 1.1 copy.79
  176.7 4.2 %all-to-all-start = ((f32[16,4,4,512]{3,2,1,0:T(4,128)}), f32[16,4,4,512]{3,2,1,0:T(4,128)S(1)}, u32[]{:S(2)}, u32[]{:S(2)}) async-start(f32[16,4,4,512]{3,2,1,0:T(4,128)} %copy.79), calls=%async_computation | async-start | bytes 1048576 | tf_op jit(solution)/shard_map/all_to_all | solution.py:38
  180.9 0.7 all_to_all.28
  181.5 13.4 %all-to-all-done = f32[16,4,4,512]{3,2,1,0:T(4,128)S(1)} async-done(((f32[16,4,4,512]{3,2,1,0:T(4,128)}), f32[16,4,4,512]{3,2,1,0:T(4,128)S(1)}, u32[]{:S(2)}, u32[]{:S(2)}) %all-to-all-start) | async-done | bytes 524320 | tf_op jit(solution)/shard_map/all_to_all | solution.py:38
  195.0 0.1 fusion.22
  195.2 0.1 reduce_sum.106
  195.5 0.6 pad_maximum_fusion.1
  (29 shorter events, 0.8 us)
Async XLA Ops:
  7.2 106.4 %all-gather.3.cloned.1.call-start = ((), (), s32[]{:S(2)}) async-start(), calls=%async_computation.3 | async-start | bytes 4456448 | tf_op jit(solution)/shard_map/all_gather | solution.py:19
  9.3 29.3 %all-to-all-start.1 = ((s32[2,64,2]{2,0,1:T(2,128)}), s32[2,64,2]{2,0,1:T(2,128)S(1)}, u32[]{:S(2)}, u32[]{:S(2)}) async-start(s32[2,64,2]{2,0,1:T(2,128)} %copy.87), calls=%async_computation.1 | async-start | bytes 131072 | tf_op jit(solution)/shard_map/all_to_all | solution.py:55
  39.0 74.6 %copy-start = (bf16[4,510,256]{2,0,1:T(4,128)(2,1)S(1)}, bf16[4,510,256]{2,0,1:T(4,128)(2,1)}, u32[]{:S(2)}) copy-start(bf16[4,510,256]{2,0,1:T(4,128)(2,1)} %param.8) | copy-start | bytes 3133444
  44.3 132.3 %all-to-all-start.2 = ((f32[2,4,32]{1,0,2:T(2,128)}), f32[2,4,32]{1,0,2:T(2,128)S(1)}, u32[]{:S(2)}, u32[]{:S(2)}) async-start(f32[2,4,32]{1,0,2:T(2,128)} %copy.93), calls=%async_computation.2 | async-start | bytes 65536 | tf_op jit(solution)/shard_map/all_to_all | solution.py:85
  176.7 18.3 %all-to-all-start = ((f32[16,4,4,512]{3,2,1,0:T(4,128)}), f32[16,4,4,512]{3,2,1,0:T(4,128)S(1)}, u32[]{:S(2)}, u32[]{:S(2)}) async-start(f32[16,4,4,512]{3,2,1,0:T(4,128)} %copy.79), calls=%async_computation | async-start | bytes 1048576 | tf_op jit(solution)/shard_map/all_to_all | solution.py:38
Sparse Core Ops, SparseCore 0:
  10.6 102.9 all-gather.2
where the time goes:
time: 203 us
  waiting for transfers between devices  77.4 us (38%)
  other arithmetic  38.6 us (19%)
  matrix products  29.9 us (15%)
  blocking collectives  17.5 us (9%)
  starting transfers between devices  16.1 us (8%)
  between operations  14.2 us (7%)
  local copies, waits for them, and re-layouts  9.39 us (5%)
    all_gather x1, waiting for transfers between devices, coarse(): lax.all_gather(coarse_query.reshape(track_group * heads, channels), 'blk'...  63.3 us
    reduce_sum x1, other arithmetic, coarse(): jnp.sum(weights, axis=2)  36.5 us
    dot_general x1, matrix products, coarse(): jnp.einsum('brc,fpc->bfpr', queries, coarse_feat, preferred_element_type=...  25.3 us
    all_gather x1, blocking collectives, fine(): descs = lax.all_gather(fine_query, 'frames', axis=0, tiled=True)  17.5 us
    all_to_all x1, waiting for transfers between devices, coarse(): lax.all_to_all(stats, 'blk', split_axis=0, concat_axis=0, tiled=True)  13.4 us
    all_to_all x1, starting transfers between devices, fine(): lax.all_to_all(out, 'frames', split_axis=2, concat_axis=1, tiled=True)  5.99 us
    all_to_all x1, starting transfers between devices, fine(): lax.all_to_all(track_pos, 'frames', split_axis=1, concat_axis=2, tiled=True)  5.86 us
    sub x1, matrix products, fine(): weights = jnp.exp(scores - jnp.max(scores, axis=2, keepdims=True))  4.61 us
  transfers between devices with their start and end apart: 4, of which 2 were waited for; matrix products, arithmetic and copies ran while one was open for 37% of the time, Pallas kernels for 0%

commit v1 on v0

--- a/solution.py
+++ b/solution.py
@@ -82,7 +82,10 @@
             jnp.sum(weights * away_col, axis=2) / total / SPREAD,
         ]
     )
-    return lax.all_to_all(out, "frames", split_axis=2, concat_axis=1, tiled=True)
+    return jnp.concatenate(
+        lax.all_to_all(jnp.stack(jnp.split(out, lax.axis_size("frames"), axis=2)), "frames", 0, 0),
+        axis=1,
+    )
 
 
 def body(coarse_query, coarse_feat, fine_query, fine_tiles, track_pos, tile_list, tile_valid):

time: 203 us -> 204 us (level)
  local copies, waits for them, and re-layouts: 9.39 us -> 19.6 us
  waiting for transfers between devices: 77.4 us -> 67.8 us
    all_gather x1, waiting for transfers between devices: 63.3 us -> 53.2 us  [coarse(): lax.all_gather(coarse_query.reshape(track_group * heads, channels), 'blk'...]
    unnamed x3 -> x18, local copies, waits for them, and re-layouts: 1.41 us -> 10.2 us
  transfers between devices with their start and end apart: 4 -> 4, of which waited for: 2 -> 2; matrix products, arithmetic and copies ran while one was open for 37% -> 43% of each run, Pallas kernels for 0% -> 0%
where the time goes in v1:
time: 204 us
  waiting for transfers between devices  67.8 us (33%)
  other arithmetic  38.6 us (19%)
  matrix products  30 us (15%)
  local copies, waits for them, and re-layouts  19.6 us (10%)
  blocking collectives  17.5 us (9%)
  starting transfers between devices  16.1 us (8%)
  between operations  14.2 us (7%)
    all_gather x1, waiting for transfers between devices, coarse(): lax.all_gather(coarse_query.reshape(track_group * heads, channels), 'blk'...  53.2 us
    reduce_sum x1, other arithmetic, coarse(): jnp.sum(weights, axis=2)  36.4 us
    dot_general x1, matrix products, coarse(): jnp.einsum('brc,fpc->bfpr', queries, coarse_feat, preferred_element_type=...  25.3 us
    all_gather x1, blocking collectives, fine(): descs = lax.all_gather(fine_query, 'frames', axis=0, tiled=True)  17.5 us
    all_to_all x1, waiting for transfers between devices, coarse(): lax.all_to_all(stats, 'blk', split_axis=0, concat_axis=0, tiled=True)  13.9 us
    unnamed x18, local copies, waits for them, and re-layouts  10.2 us
    all_to_all x1, starting transfers between devices, fine(): lax.all_to_all(jnp.stack(jnp.split(out, lax.axis_size('frames'), axis=2))...  5.99 us
    all_to_all x1, starting transfers between devices, fine(): lax.all_to_all(track_pos, 'frames', split_axis=1, concat_axis=2, tiled=True)  5.86 us
  transfers between devices with their start and end apart: 4, of which 2 were waited for; matrix products, arithmetic and copies ran while one was open for 43% of the time, Pallas kernels for 0%

profile of v1, /device:TPU:2, one launch (start us, length us, event | category | flops | bytes accessed | tf_op | source)
XLA Modules:
  0.0 203.7 jit_solution(10711308256486588614)
XLA Ops:
  7.2 0.7 all-gather.3.cloned.1.call-update
  7.9 1.4 copy.192
  9.3 5.9 %all-to-all-start.1 = ((s32[2,64,2]{2,0,1:T(2,128)}), s32[2,64,2]{2,0,1:T(2,128)S(1)}, u32[]{:S(2)}, u32[]{:S(2)}) async-start(s32[2,64,2]{2,0,1:T(2,128)} %copy.192), calls=%async_computation.1 | async-start | bytes 131072 | tf_op jit(solution)/shard_map/all_to_all | solution.py:55
  15.2 0.8 copy.188
  16.0 0.7 compare_bitcast_fusion
  17.1 17.5 %all-gather = bf16[16,2,128]{2,1,0:T(2,128)(2,1)S(1)} all-gather(bf16[1,2,128]{2,1,0:T(2,128)(2,1)} %bitcast.141), channel_id=1, replica_groups=mesh['blk'=16,'frames'=16] {'frames'}, dimensions={0}, use_global_device_ids=true | all-gather | bytes 8704 | tf_op jit(solution)/shard_map/all_gather | solution.py:54
  34.6 1.4 broadcast_in_dim.9
  36.0 2.7 %reshape.208 = pred[4,32,4096]{2,1,0:T(32,128)(4,1)S(1)} reshape(pred[4,32,64,64]{3,2,1,0:T(32,128)(4,1)S(1)} %broadcast_in_dim.9) | data formatting | bytes 1048576 | tf_op jit(solution)/shard_map/reshape | solution.py:67
  39.0 4.6 %fusion.13 = (f32[4,32]{1,0:T(4,128)S(1)}, f32[4,32]{1,0:T(4,128)S(1)}, f32[4,32]{1,0:T(4,128)S(1)}) fusion(f32[4,32]{1,0:T(4,128)S(1)} %copy.197, f32[4096]{0:T(1024)S(1)} %get-tuple-element.36, f32[4,32]{1,0:T(4,128)S(1)} %copy.195, f32[4096]{0:T(1024)S(1)} %get-tuple-element.35, pred[4,32,4096]{2,1,0:T(32,128)(4,1)S(1)} %reshape.208, ...), kind=kOutput, calls=%fused_computation.22 | convolution fusion | flops 143134464 | bytes 4762112 | tf_op jit(solution)/shard_map/sub | solution.py:77
  45.4 0.6 constant_dynamic-update-slice_fusion.15
  46.0 0.6 constant_dynamic-update-slice_fusion.14
  47.2 0.6 constant_dynamic-update-slice_fusion.12
  47.8 0.6 constant_dynamic-update-slice_fusion.11
  52.4 0.6 constant_dynamic-update-slice_fusion.3
  53.6 0.6 constant_dynamic-update-slice_fusion.1
  54.8 6.0 %all-to-all-start.2 = ((f32[16,2,4,2]{2,3,1,0:T(2,128)}), f32[16,2,4,2]{2,3,1,0:T(2,128)S(1)}, u32[]{:S(2)}, u32[]{:S(2)}) async-start(f32[16,2,4,2]{2,3,1,0:T(2,128)} %constant_dynamic-update-slice_fusion), calls=%async_computation.2 | async-start | bytes 65536 | tf_op jit(solution)/shard_map/all_to_all | solution.py:86
  60.8 53.2 %all-gather.3.cloned.1.call-done = bf16[16,512,256]{2,1,0:T(8,128)(2,1)} async-done(((bf16[1,512,256]{2,1,0:T(8,128)(2,1)}), bf16[16,512,256]{2,1,0:T(8,128)(2,1)}) %all-gather.3.cloned.1.call-update) | async-done | bytes 4194320 | tf_op jit(solution)/shard_map/all_gather | solution.py:19
  113.9 25.3 %bitcast_reduce_fusion = (f32[16,4,512]{2,0,1:T(8,128)S(1)}, f32[4,510,16,512]{3,1,2,0:T(8,128)}) fusion(bf16[16,512,256]{2,1,0:T(8,128)(2,1)} %all-gather.3.cloned.1.call-done, bf16[4,510,256,1]{2,0,1,3:T(4,128)(2,1)S(1)} %bitcast.129), kind=kOutput, calls=%fused_computation.2 | convolution fusion | flops 8589770752 | bytes 72216576 | tf_op jit(solution)/shard_map/brc,fpc->bfpr/dot_general | solution.py:24
  139.3 36.4 %fusion.2 = (f32[16,4,512]{2,0,1:T(8,128)S(1)}, f32[16,4,512]{2,0,1:T(8,128)S(1)}, f32[16,4,512]{2,0,1:T(8,128)S(1)}) fusion(f32[4,510,16,512]{3,1,2,0:T(8,128)} %get-tuple-element.34, f32[16,4,512]{2,0,1:T(8,128)S(1)} %get-tuple-element.33, f32[510]{0:T(512)S(1)} %get-tuple-element.38, f32[510]{0:T(512)S(1)} %get-tuple-element.37), kind=kLoop, calls=%fused_computation.6 | loop fusion | flops 116883456 | bytes 67375088 | tf_op jit(solution)/shard_map/reduce_sum | solution.py:32
  175.7 1.1 copy.184
  176.9 4.2 %all-to-all-start = ((f32[16,4,4,512]{3,2,1,0:T(4,128)}), f32[16,4,4,512]{3,2,1,0:T(4,128)S(1)}, u32[]{:S(2)}, u32[]{:S(2)}) async-start(f32[16,4,4,512]{3,2,1,0:T(4,128)} %copy.184), calls=%async_computation | async-start | bytes 1048576 | tf_op jit(solution)/shard_map/all_to_all | solution.py:38
  181.1 0.7 reshape.211
  181.8 13.9 %all-to-all-done = f32[16,4,4,512]{3,2,1,0:T(4,128)S(1)} async-done(((f32[16,4,4,512]{3,2,1,0:T(4,128)}), f32[16,4,4,512]{3,2,1,0:T(4,128)S(1)}, u32[]{:S(2)}, u32[]{:S(2)}) %all-to-all-start) | async-done | bytes 524320 | tf_op jit(solution)/shard_map/all_to_all | solution.py:38
  196.3 0.6 pad_maximum_fusion.2
  (60 shorter events, 8.9 us)
Async XLA Ops:
  7.2 106.8 %all-gather.3.cloned.1.call-start = ((), (), s32[]{:S(2)}) async-start(), calls=%async_computation.3 | async-start | bytes 4456448 | tf_op jit(solution)/shard_map/all_gather | solution.py:19
  9.3 29.3 %all-to-all-start.1 = ((s32[2,64,2]{2,0,1:T(2,128)}), s32[2,64,2]{2,0,1:T(2,128)S(1)}, u32[]{:S(2)}, u32[]{:S(2)}) async-start(s32[2,64,2]{2,0,1:T(2,128)} %copy.192), calls=%async_computation.1 | async-start | bytes 131072 | tf_op jit(solution)/shard_map/all_to_all | solution.py:55
  39.0 74.9 %copy-start = (bf16[4,510,256]{2,0,1:T(4,128)(2,1)S(1)}, bf16[4,510,256]{2,0,1:T(4,128)(2,1)}, u32[]{:S(2)}) copy-start(bf16[4,510,256]{2,0,1:T(4,128)(2,1)} %param.8) | copy-start | bytes 3133444
  54.8 122.1 %all-to-all-start.2 = ((f32[16,2,4,2]{2,3,1,0:T(2,128)}), f32[16,2,4,2]{2,3,1,0:T(2,128)S(1)}, u32[]{:S(2)}, u32[]{:S(2)}) async-start(f32[16,2,4,2]{2,3,1,0:T(2,128)} %constant_dynamic-update-slice_fusion), calls=%async_computation.2 | async-start | bytes 65536 | tf_op jit(solution)/shard_map/all_to_all | solution.py:86
  176.9 18.8 %all-to-all-start = ((f32[16,4,4,512]{3,2,1,0:T(4,128)}), f32[16,4,4,512]{3,2,1,0:T(4,128)S(1)}, u32[]{:S(2)}, u32[]{:S(2)}) async-start(f32[16,4,4,512]{3,2,1,0:T(4,128)} %copy.184), calls=%async_computation | async-start | bytes 1048576 | tf_op jit(solution)/shard_map/all_to_all | solution.py:38
Sparse Core Ops, SparseCore 0:
  10.6 103.2 all-gather.2
